TPU v7x, 32 devices: a whole 2x2x4 slice. The times are simulated.
32 devices in a mesh: rows: 8 (over z, x), feat: 4 (over y, core).
Axes of the slice: x: 2, y: 2, z: 4, core: 2. Of those that a mesh axis runs over, the one named last changes fastest.
Arguments:
- samples: float32 [8192, 440], P(('rows', 'feat')), may hold values from -6 to 6
- residual: float32 [8192, 147], P(('rows', 'feat')), may hold values from -4 to 4
- projections: float32 [8, 440, 1024], P('feat'), may hold values from -0.4375 to 0.4375
- phases: float32 [8, 1024], P('feat'), may hold values from 0 to 6.2831855
- weights: float32 [8, 1024, 147], P('feat'), may hold values from -4 to 4
- block_order: int32 [8], replicated, may hold values from 0 to 7, each once
Outputs:
- residual_out: float32 [8192, 147], P(('rows', 'feat'))
- new_weights: float32 [1, 1024, 147], replicated
Inputs may be any that keep to these rules, and one draw needn't show every extreme that they name: Block k is held by index k // 2 of feat; the blocks updated are those of the first 1 entries of block_order.
All inputs are finite; a program needn't handle non-finite values.
Results may differ from a plain program's by a relative error of at most 0.0003.
Values sent between devices are 32-bit elements; how exact they have to be, the bound alone decides.
A program may use at most 128 MiB of HBM per device.

v0:
```python
import jax
import jax.numpy as jnp
from jax import lax
from jax.sharding import PartitionSpec as P

root_two = 1.4142135623730951
penalty = 0.05


def from_root(block, axis, holder):
    block = jnp.where(lax.axis_index(axis) == holder, block, jnp.zeros_like(block))
    return lax.psum(block, axis)


def body(samples, residual, projections, phases, weights, block_order):
    per_device = projections.shape[0]
    block_width = projections.shape[2]
    devices = lax.axis_size("rows") * lax.axis_size("feat")
    total_rows = samples.shape[0] * devices
    block_id = block_order[0]
    owner_index = block_id // per_device
    slot_index = block_id % per_device
    local_block = (
        lax.dynamic_index_in_dim(projections, slot_index, 0, False),
        lax.dynamic_index_in_dim(phases, slot_index, 0, False),
        lax.dynamic_index_in_dim(weights, slot_index, 0, False),
    )
    basis_block = from_root(local_block[0], "feat", owner_index)
    phase_block = from_root(local_block[1], "feat", owner_index)
    old_weights = from_root(local_block[2], "feat", owner_index)
    projected = jnp.dot(
        samples, basis_block, precision=lax.Precision.HIGHEST, preferred_element_type=jnp.float32
    )
    features = root_two * jnp.cos(projected + phase_block)
    joined = jnp.concatenate([features, residual], axis=1)
    share_rows = lax.psum_scatter(
        lax.dot_general(
            features,
            joined,
            (((0,), (0,)), ((), ())),
            precision=lax.Precision.HIGHEST,
            preferred_element_type=jnp.float32,
        ),
        "rows",
        scatter_dimension=0,
        tiled=True,
    )
    share_rows = lax.psum(share_rows, "feat")
    summed = lax.all_gather(share_rows, "rows", axis=0, tiled=True)
    gram_sum = summed[:, :block_width]
    cross_sum = summed[:, block_width:]
    gram_matrix = gram_sum / total_rows
    cross_term = cross_sum / total_rows
    system = gram_matrix + penalty * jnp.eye(block_width, dtype=jnp.float32)
    factor = jnp.linalg.cholesky(system)
    change = jax.scipy.linalg.cho_solve((factor, True), cross_term - penalty * old_weights)
    results = [old_weights + change]
    residual = residual - jnp.dot(
        features, change, precision=lax.Precision.HIGHEST, preferred_element_type=jnp.float32
    )
    return (residual, jnp.stack(results))


def solution(mesh):
    return jax.shard_map(
        body,
        mesh=mesh,
        in_specs=(
            P(("rows", "feat"), None),
            P(("rows", "feat"), None),
            P("feat", None, None),
            P("feat", None),
            P("feat", None, None),
            P(),
        ),
        out_specs=(P(("rows", "feat"), None), P()),
        check_vma=False,
    )
```

profile of v0, /device:TPU:0, one launch (start us, length us, event | category | flops | bytes accessed | tf_op | source)
XLA Modules:
  0.0 661.0 jit_solution(17731354791769132694)
XLA Ops:
  10.0 3.0 select_bitcast_fusion
  13.1 8.4 %psum.29 = f32[1024]{0:T(1024)S(1)} all-reduce(f32[1024]{0:T(1024)S(1)} %bitcast.141), channel_id=1, replica_groups=mesh['rows'=8,'feat'=4] {'feat'}, use_global_device_ids=true, to_apply=%region_1.2 | all-reduce | flops 1024 | bytes 8192 | tf_op jit(solution)/shard_map/psum | solution.py:12
  21.4 41.0 %all-reduce.5.cloned.1.call-done = f32[440,1024]{1,0:T(8,128)} async-done(((f32[440,1024]{1,0:T(8,128)}), f32[440,1024]{1,0:T(8,128)}) %all-reduce.5.cloned.1.call-update) | async-done | bytes 1802256 | tf_op jit(solution)/shard_map/psum | solution.py:12
  62.4 8.3 %fusion.3 = f32[1024,256]{1,0:T(8,128)S(1)} fusion(f32[440,1024]{1,0:T(8,128)} %all-reduce.5.cloned.1.call-done, f32[256,440]{0,1:T(8,128)S(1)} %copy-done.9, f32[1024]{0:T(1024)S(1)} %psum.29), kind=kOutput, calls=%fused_computation.12 | convolution fusion | flops 1384644608 | bytes 3305472 | tf_op jit(solution)/shard_map/dot_general | solution.py:31
  70.7 5.8 fusion.4
  78.2 95.5 %reduce-scatter.2.cloned.1.call-done = f32[128,1171]{0,1:T(8,128)} async-done(((f32[1024,1171]{0,1:T(8,128)}), f32[128,1171]{0,1:T(8,128)}) %reduce-scatter.2.cloned.1.call-update) | async-done | bytes 599568 | tf_op jit(solution)/shard_map/reduce_scatter | solution.py:36
  173.8 39.9 %all-reduce.7.cloned.1.call-done = (f32[128,1171]{0,1:T(8,128)}, f32[1024,147]{0,1:T(8,128)}) async-done(((f32[128,1171]{0,1:T(8,128)}, f32[1024,147]{0,1:T(8,128)}), (f32[128,1171]{0,1:T(8,128)}, f32[1024,147]{0,1:T(8,128)})) %all-reduce.7.cloned.1.call-update) | async-done | bytes 1201680 | tf_op jit(solution)/shard_map/psum | solution.py:48
  213.7 84.1 %all-gather.2.cloned.1.call-done = f32[1024,1171]{0,1:T(8,128)} async-done(((f32[128,1171]{0,1:T(8,128)}), f32[1024,1171]{0,1:T(8,128)}) %all-gather.2.cloned.1.call-update) | async-done | bytes 4796432 | tf_op jit(solution)/shard_map/all_gather | solution.py:49
  297.8 5.1 fusion
  302.8 5.5 copy.8
  308.4 4.5 fusion.1
  312.9 2.0 copy-done.3
  314.9 11.7 %cholesky.222 = f32[128,128]{1,0:T(8,128)S(1)} custom-call(f32[128,128]{1,0:T(8,128)S(1)} %cholesky.577), custom_call_target="Cholesky" | custom-call | tf_op jit(solution)/shard_map/jit(cholesky)/cholesky | solution.py:55
  326.7 9.8 %custom-call.66 = f32[1,128,128]{1,2,0:T(8,128)S(1)} custom-call(f32[1,128,128]{2,1,0:T(8,128)S(1)} %get-tuple-element.58), custom_call_target="InvertDiagBlocksLowerTriangular" | custom-call | tf_op jit(solution)/shard_map/jit(cholesky)/cholesky | solution.py:55
  336.5 1.5 fusion.18
  338.3 1.6 convolution_subtract_fusion
  340.7 11.7 %cholesky.243 = f32[128,128]{1,0:T(8,128)S(1)} custom-call(f32[128,128]{1,0:T(8,128)S(1)} %cholesky.581), custom_call_target="Cholesky" | custom-call | tf_op jit(solution)/shard_map/jit(cholesky)/cholesky | solution.py:55
  352.7 9.8 %custom-call.67 = f32[1,128,128]{1,2,0:T(8,128)S(1)} custom-call(f32[1,128,128]{2,1,0:T(8,128)S(1)} %get-tuple-element.56), custom_call_target="InvertDiagBlocksLowerTriangular" | custom-call | tf_op jit(solution)/shard_map/jit(cholesky)/cholesky | solution.py:55
  363.7 2.0 copy-done.1
  365.7 2.4 convolution_subtract_fusion.1
  368.1 11.7 %cholesky.466 = f32[128,128]{1,0:T(8,128)S(1)} custom-call(f32[128,128]{1,0:T(8,128)S(1)} %cholesky.586), custom_call_target="Cholesky" | custom-call | tf_op jit(solution)/shard_map/jit(cholesky)/cholesky | solution.py:55
  380.6 9.8 %custom-call.68 = f32[1,128,128]{1,2,0:T(8,128)S(1)} custom-call(f32[1,128,128]{2,1,0:T(8,128)S(1)} %get-tuple-element.54), custom_call_target="InvertDiagBlocksLowerTriangular" | custom-call | tf_op jit(solution)/shard_map/jit(cholesky)/cholesky | solution.py:55
  391.6 3.6 convolution_subtract_fusion.2
  395.2 11.7 %cholesky.485 = f32[128,128]{1,0:T(8,128)S(1)} custom-call(f32[128,128]{1,0:T(8,128)S(1)} %cholesky.591), custom_call_target="Cholesky" | custom-call | tf_op jit(solution)/shard_map/jit(cholesky)/cholesky | solution.py:55
  407.7 9.8 %custom-call.69 = f32[1,128,128]{1,2,0:T(8,128)S(1)} custom-call(f32[1,128,128]{2,1,0:T(8,128)S(1)} %get-tuple-element.52), custom_call_target="InvertDiagBlocksLowerTriangular" | custom-call | tf_op jit(solution)/shard_map/jit(cholesky)/cholesky | solution.py:55
  418.6 3.2 convolution_subtract_fusion.3
  421.8 11.9 %cholesky.504 = f32[128,128]{1,0:T(8,128)S(1)} custom-call(f32[128,128]{1,0:T(8,128)S(1)} %cholesky.596), custom_call_target="Cholesky" | custom-call | tf_op jit(solution)/shard_map/jit(cholesky)/cholesky | solution.py:55
  434.5 9.8 %custom-call.70 = f32[1,128,128]{1,2,0:T(8,128)S(1)} custom-call(f32[1,128,128]{2,1,0:T(8,128)S(1)} %get-tuple-element.50), custom_call_target="InvertDiagBlocksLowerTriangular" | custom-call | tf_op jit(solution)/shard_map/jit(cholesky)/cholesky | solution.py:55
  445.4 3.2 convolution_subtract_fusion.4
  448.6 11.7 %cholesky.524 = f32[128,128]{1,0:T(8,128)S(1)} custom-call(f32[128,128]{1,0:T(8,128)S(1)} %cholesky.601), custom_call_target="Cholesky" | custom-call | tf_op jit(solution)/shard_map/jit(cholesky)/cholesky | solution.py:55
  461.1 9.8 %custom-call.71 = f32[1,128,128]{1,2,0:T(8,128)S(1)} custom-call(f32[1,128,128]{2,1,0:T(8,128)S(1)} %get-tuple-element.48), custom_call_target="InvertDiagBlocksLowerTriangular" | custom-call | tf_op jit(solution)/shard_map/jit(cholesky)/cholesky | solution.py:55
  471.9 3.1 convolution_subtract_fusion.6
  475.0 11.7 %cholesky.544 = f32[128,128]{1,0:T(8,128)S(1)} custom-call(f32[128,128]{1,0:T(8,128)S(1)} %cholesky.606), custom_call_target="Cholesky" | custom-call | tf_op jit(solution)/shard_map/jit(cholesky)/cholesky | solution.py:55
  487.5 9.8 %custom-call.72 = f32[1,128,128]{1,2,0:T(8,128)S(1)} custom-call(f32[1,128,128]{2,1,0:T(8,128)S(1)} %get-tuple-element.46), custom_call_target="InvertDiagBlocksLowerTriangular" | custom-call | tf_op jit(solution)/shard_map/jit(cholesky)/cholesky | solution.py:55
  498.3 2.1 convolution_subtract_fusion.21
  500.4 11.7 %cholesky.562 = f32[128,128]{1,0:T(8,128)S(1)} custom-call(f32[128,128]{1,0:T(8,128)S(1)} %convolution_subtract_fusion.21), custom_call_target="Cholesky" | custom-call | tf_op jit(solution)/shard_map/jit(cholesky)/cholesky | solution.py:55
  522.8 5.0 select_select_fusion
  527.8 28.3 %while.1 = (s32[]{:T(128)}, f32[1024,1024]{0,1:T(8,128)}, s32[8,2]{0,1:T(2,128)S(1)}, f32[8,128,128]{2,1,0:T(8,128)}, s32[]{:T(128)}) while((s32[]{:T(128)}, f32[1024,1024]{0,1:T(8,128)}, s32[8,2]{0,1:T(2,128)S(1)}, f32[8,128,128]{2,1,0:T(8,128)}, s32[]{:T(128)}) %tuple.54), condition=%wide.while_cond, body=%wide.while_body.sunk | while | flops 2 | bytes 393329 | solution.py:56
  528.4 2.2 dynamic-slice.7
  531.9 2.2 dynamic-slice.7
  535.5 2.2 dynamic-slice.7
  539.0 2.2 dynamic-slice.7
  542.6 2.2 dynamic-slice.7
  546.1 2.2 dynamic-slice.7
  549.6 2.2 dynamic-slice.7
  553.2 2.1 dynamic-slice.7
  556.1 79.5 %custom-call.73 = f32[8,128,128]{1,2,0:T(8,128)S(1)} custom-call(f32[8,128,128]{2,1,0:T(8,128)} %get-tuple-element.9), custom_call_target="InvertDiagBlocksLowerTriangular" | custom-call | tf_op jit(solution)/shard_map/jit(_cho_solve)/triangular_solve | solution.py:56
  651.3 1.5 convolution_subtract_fusion.5
  (167 shorter events, 46.7 us)
Async XLA Ops:
  7.2 69.4 %copy-start = (f32[2,1024,147]{1,0,2:T(2,128)S(1)}, f32[2,1024,147]{1,0,2:T(2,128)}, u32[]{:S(2)}) copy-start(f32[2,1024,147]{1,0,2:T(2,128)} %param.10) | copy-start | bytes 3612676
  7.2 5.9 copy-start.10
  7.2 55.2 %copy-start.9 = (f32[256,440]{0,1:T(8,128)S(1)}, f32[256,440]{0,1:T(8,128)}, u32[]{:S(2)}) copy-start(f32[256,440]{0,1:T(8,128)} %param.6) | copy-start | bytes 1351684
  7.2 55.2 %all-reduce.5.cloned.1.call-start = ((), (), s32[]{:S(2)}) async-start(), calls=%async_computation.1 | async-start | bytes 3604480 | tf_op jit(solution)/shard_map/psum | solution.py:12
  10.0 60.8 %copy-start.7 = (f32[256,147]{0,1:T(8,128)S(1)}, f32[256,147]{0,1:T(8,128)}, u32[]{:S(2)}) copy-start(f32[256,147]{0,1:T(8,128)} %param.7) | copy-start | bytes 451588
  13.0 160.7 %reduce-scatter.2.cloned.1.call-start = ((), (), s32[]{:S(2)}) async-start(), calls=%async_computation.2 | async-start | bytes 5419008 | tf_op jit(solution)/shard_map/reduce_scatter | solution.py:36
  76.6 137.1 %all-reduce.7.cloned.1.call-start = ((), (), s32[]{:S(2)}) async-start(), calls=%async_computation.4 | async-start | bytes 2449408 | tf_op jit(solution)/shard_map/psum | solution.py:48
  173.7 124.0 %all-gather.2.cloned.1.call-start = ((), (), s32[]{:S(2)}) async-start(), calls=%async_computation.3 | async-start | bytes 5419008 | tf_op jit(solution)/shard_map/all_gather | solution.py:49
  312.8 2.0 copy-start.3
  339.8 0.8 copy-start.5
  340.7 22.5 %copy-start.6 = (f32[896,128]{1,0:T(8,128)S(1)}, f32[896,128]{1,0:T(8,128)}, u32[]{:S(2)}) copy-start(f32[896,128]{1,0:T(8,128)} %copy-done.5) | copy-start | bytes 1376260
  363.7 2.0 copy-start.1
  522.8 112.8 %copy-start.4 = (f32[1024,147]{0,1:T(8,128)S(1)}, f32[1024,147]{0,1:T(8,128)}, u32[]{:S(2)}) copy-start(f32[1024,147]{0,1:T(8,128)} %get-tuple-element.25) | copy-start | bytes 1806340
  635.6 6.2 copy-start.2
  647.6 3.8 copy-start.8
Sparse Core Ops, SparseCore 0:
  13.1 49.2 all-reduce.4
  76.7 96.9 reduce-scatter.1
  176.3 37.2 all-reduce.6
  215.5 82.1 all-gather.1
where the time goes:
time: 667 us; the launch traced here: 661 us
  other arithmetic  267 us (40%)
  waiting for transfers between devices  261 us (39%)
  matrix products  55.8 us (8%)
  local copies, waits for them, and re-layouts  46.3 us (7%)
  between operations  22.6 us (3%)
  blocking collectives  8.38 us (1%)
    another operation x30, other arithmetic, body(): factor = jnp.linalg.cholesky(system)  168 us
    reduce_scatter x1, waiting for transfers between devices, body(): lax.psum_scatter(lax.dot_general(features, joined, (((0,), (0,)), ((), ()...  95.5 us
    another operation x3, other arithmetic, body(): jax.scipy.linalg.cho_solve((factor, True), cross_term - penalty * old_wei...  84.5 us
    all_gather x1, waiting for transfers between devices, body(): summed = lax.all_gather(share_rows, 'rows', axis=0, tiled=True)  84.1 us
    psum x1, waiting for transfers between devices, from_root(): return lax.psum(block, axis)  41 us
    psum x1, waiting for transfers between devices, body(): share_rows = lax.psum(share_rows, 'feat')  39.9 us
    another operation x40, local copies, waits for them, and re-layouts  28.1 us
    another operation x14, matrix products, body(): factor = jnp.linalg.cholesky(system)  26.5 us
  transfers between devices with their start and end apart: 4, of which 4 were waited for; matrix products, arithmetic and copies ran while one was open for 0% of the time, Pallas kernels for 0%

commit v1 on v0

v1 whole, which is shorter than its diff:
```python
import functools

import jax
import jax.numpy as jnp
from jax import lax
from jax.experimental import pallas as pl
from jax.experimental.pallas import tpu as pltpu
from jax.sharding import PartitionSpec as P

root_two = 1.4142135623730951
penalty = 0.05
LANES = 128
HIGHEST = lax.Precision.HIGHEST
VMEM_LIMIT = 48 * 1024 * 1024


def round_up(value, step):
    return -(-value // step) * step


def dot_nt(left, right):
    return lax.dot_general(
        left, right, (((1,), (1,)), ((), ())), precision=HIGHEST, preferred_element_type=jnp.float32
    )


def dot_nn(left, right):
    return lax.dot_general(
        left, right, (((1,), (0,)), ((), ())), precision=HIGHEST, preferred_element_type=jnp.float32
    )


def axis_bits(name, size):
    bits, step = [], 1
    while step < size:
        bits.append((name, step))
        step *= 2
    return bits


def greet(bits):
    barrier = pltpu.get_barrier_semaphore()
    for name, step in bits:
        me = lax.axis_index(name)
        partner = me + step * (1 - 2 * ((me // step) % 2))
        pl.semaphore_signal(
            barrier, inc=1, device_id={name: partner}, device_id_type=pl.DeviceIdType.MESH
        )
    pl.semaphore_wait(barrier, len(bits))


def sum_over(plans, buf, recv, out, send_sems, recv_sems):
    rows_of = lambda start, size: pl.ds(pl.multiple_of(start, 8), size)
    state = [(base, rows) for base, rows, _ in plans]
    landing = [base for base, _, _ in plans]
    count = len(plans[0][2])

    def peer(part, step):
        name, stride = plans[part][2][step]
        me = lax.axis_index(name)
        bit = (me // stride) % 2
        return name, me + stride * (1 - 2 * bit), bit

    for step in range(count):
        copies = []
        for part in range(len(plans)):
            name, partner, bit = peer(part, step)
            start, size = state[part]
            half = size // 2
            copy = pltpu.make_async_remote_copy(
                src_ref=buf.at[rows_of(start + (1 - bit) * half, half)],
                dst_ref=recv.at[pl.ds(landing[part], half)],
                send_sem=send_sems.at[0, part, step],
                recv_sem=recv_sems.at[0, part, step],
                device_id={name: partner},
                device_id_type=pl.DeviceIdType.MESH,
            )
            copy.start()
            copies.append(copy)
            state[part] = (start + bit * half, half)
        for part, copy in enumerate(copies):
            copy.wait()
            start, half = state[part]
            mine = rows_of(start, half)
            buf[mine, :] = buf[mine, :] + recv[pl.ds(landing[part], half), :]
            landing[part] += half
    for start, size in state:
        mine = rows_of(start, size)
        out[mine, :] = buf[mine, :]
    for step in reversed(range(count)):
        copies = []
        for part in range(len(plans)):
            name, partner, bit = peer(part, step)
            start, size = state[part]
            mine = rows_of(start, size)
            copy = pltpu.make_async_remote_copy(
                src_ref=out.at[mine],
                dst_ref=out.at[mine],
                send_sem=send_sems.at[1, part, step],
                recv_sem=recv_sems.at[1, part, step],
                device_id={name: partner},
                device_id_type=pl.DeviceIdType.MESH,
            )
            copy.start()
            copies.append(copy)
            state[part] = (start - bit * size, size * 2)
        for copy in copies:
            copy.wait()


def spread_kernel(bits, plans, block_ref, out_ref, buf, recv, send_sems, recv_sems):
    greet(bits)
    buf[...] = block_ref[...]
    sum_over(plans, buf, recv, out_ref, send_sems, recv_sems)


def gram_kernel(bits, plans, features_ref, targets_ref, out_ref, buf, recv, send_sems, recv_sems):
    greet(bits)
    tiles = features_ref.shape[0] // LANES
    at = 0
    for i in range(tiles):
        panel = dot_nt(features_ref[i * LANES:(i + 1) * LANES, :], features_ref[:(i + 1) * LANES, :])
        for j in range(i + 1):
            buf[at:at + LANES, :] = panel[:, j * LANES:(j + 1) * LANES]
            at += LANES
    cross = dot_nt(targets_ref[...], features_ref[...])
    depth = cross.shape[0]
    for j in range(tiles):
        buf[at:at + depth, :] = cross[:, j * LANES:(j + 1) * LANES]
        at += depth
    if at < buf.shape[0]:
        buf[at:, :] = jnp.zeros((buf.shape[0] - at, LANES), jnp.float32)
    sum_over(plans, buf, recv, out_ref, send_sems, recv_sems)


def summing_call(kernel, bits, orders, rows, operands, collective_id):
    part_rows = rows // len(orders)
    plans = [(n * part_rows, part_rows, order) for n, order in enumerate(orders)]
    sems = pltpu.SemaphoreType.DMA((2, len(orders), len(bits)))
    return pl.pallas_call(
        functools.partial(kernel, bits, plans),
        out_shape=jax.ShapeDtypeStruct((rows, LANES), jnp.float32),
        in_specs=[pl.BlockSpec(memory_space=pltpu.VMEM)] * len(operands),
        out_specs=pl.BlockSpec(memory_space=pltpu.VMEM),
        scratch_shapes=[
            pltpu.VMEM((rows, LANES), jnp.float32),
            pltpu.VMEM((rows, LANES), jnp.float32),
            sems,
            sems,
        ],
        compiler_params=pltpu.CompilerParams(
            collective_id=collective_id, has_side_effects=True, vmem_limit_bytes=VMEM_LIMIT
        ),
    )(*operands)


def invert(block):
    size = block.shape[0]
    pieces = [block[8 * n:8 * n + 8, :] for n in range(size // 8)]
    lane = lax.broadcasted_iota(jnp.int32, (1, size), 1)
    sub = lax.broadcasted_iota(jnp.int32, (8, 1), 0)
    for k in range(size):
        home, at = k // 8, k % 8
        row = pieces[home][at:at + 1, :]
        inverse = 1.0 / row[:, k:k + 1]
        scaled = row * inverse
        factor = jnp.where(lane == k, 1.0 + inverse, scaled)
        kept = jnp.where(lane == k, inverse, scaled)
        pieces = [piece - piece[:, k:k + 1] * factor for piece in pieces]
        pieces[home] = jnp.where(sub == at, kept, pieces[home])
    return jnp.concatenate(pieces, axis=0)


def solve_kernel(total_rows, packed_ref, weights_ref, change_ref, panels, diagonal_inverse):
    width = weights_ref.shape[1]
    depth = weights_ref.shape[0]
    tiles = width // LANES
    scale = 1.0 / total_rows
    eye = (
        lax.broadcasted_iota(jnp.int32, (LANES, LANES), 0)
        == lax.broadcasted_iota(jnp.int32, (LANES, LANES), 1)
    )
    at = 0
    for i in range(tiles):
        for j in range(i + 1):
            block = packed_ref[at:at + LANES, :] * scale
            if i == j:
                block = jnp.where(eye, block + penalty, block)
            panels[j, i * LANES:(i + 1) * LANES, :] = block
            at += LANES
    for j in range(tiles):
        panels[j, width:, :] = (
            packed_ref[at:at + depth, :] * scale - penalty * weights_ref[:, j * LANES:(j + 1) * LANES]
        )
        at += depth

    def eliminate(j):
        below = (j + 1) * LANES
        ratio = dot_nn(panels[j, below:, :], diagonal_inverse[...])
        for k in range(j + 1, tiles):
            panels[k, k * LANES:, :] = panels[k, k * LANES:, :] - dot_nt(
                ratio[(k - j - 1) * LANES:, :], panels[j, k * LANES:(k + 1) * LANES, :]
            )
        panels[j, below:, :] = ratio

    def step(j, carry):
        diagonal_inverse[...] = invert(panels[j, pl.ds(pl.multiple_of(j * LANES, LANES), LANES), :])
        for n in range(tiles):
            pl.when(j == n)(functools.partial(eliminate, n))
        return carry

    lax.fori_loop(0, tiles, step, 0)
    for j in reversed(range(tiles)):
        answer = panels[j, width:, :]
        if j + 1 < tiles:
            answer = answer - dot_nn(
                change_ref[:, (j + 1) * LANES:], panels[j, (j + 1) * LANES:width, :]
            )
        change_ref[:, j * LANES:(j + 1) * LANES] = answer


def body(samples, residual, projections, phases, weights, block_order):
    per_device, inputs, width = projections.shape
    classes = residual.shape[1]
    depth = round_up(classes, 8)
    feat_bits = axis_bits("feat", lax.axis_size("feat"))
    rows_bits = axis_bits("rows", lax.axis_size("rows"))
    total_rows = samples.shape[0] * lax.axis_size("rows") * lax.axis_size("feat")
    block_id = block_order[0]
    slot = block_id % per_device
    mine = lax.axis_index("feat") == block_id // per_device

    def local(array):
        block = lax.dynamic_index_in_dim(array, slot, 0, False)
        return jnp.where(mine, block, jnp.zeros_like(block))

    old_weights = lax.psum(local(weights), "feat")
    tiles = width // LANES
    spread_rows = round_up((inputs + 8) * tiles, 8 * 2 ** len(feat_bits))
    basis = jnp.concatenate(
        [local(projections), jnp.broadcast_to(local(phases)[None], (8, width))], axis=0
    ).reshape(-1, LANES)
    basis = jnp.pad(basis, ((0, spread_rows - basis.shape[0]), (0, 0)))
    spread = summing_call(spread_kernel, feat_bits, [feat_bits], spread_rows, [basis], 1)
    spread = spread[:(inputs + 8) * tiles].reshape(inputs + 8, width)
    projected = lax.dot_general(
        spread[:inputs], samples, (((0,), (1,)), ((), ())),
        precision=HIGHEST, preferred_element_type=jnp.float32,
    )
    features = root_two * jnp.cos(projected + spread[inputs][:, None])
    targets = jnp.pad(residual.T, ((0, depth - classes), (0, 0)))

    orders = [
        feat_bits + rows_bits,
        feat_bits[:1] + rows_bits[:1] + feat_bits[1:] + rows_bits[1:][::-1],
    ]
    bits = feat_bits + rows_bits
    sum_rows = round_up(
        tiles * (tiles + 1) // 2 * LANES + tiles * depth, 8 * 2 ** len(bits) * len(orders)
    )
    packed = summing_call(gram_kernel, bits, orders, sum_rows, [features, targets], 2)

    change = pl.pallas_call(
        functools.partial(solve_kernel, total_rows),
        out_shape=jax.ShapeDtypeStruct((depth, width), jnp.float32),
        in_specs=[pl.BlockSpec(memory_space=pltpu.VMEM)] * 2,
        out_specs=pl.BlockSpec(memory_space=pltpu.VMEM),
        scratch_shapes=[
            pltpu.VMEM((tiles, width + depth, LANES), jnp.float32),
            pltpu.VMEM((LANES, LANES), jnp.float32),
        ],
        compiler_params=pltpu.CompilerParams(vmem_limit_bytes=VMEM_LIMIT),
    )(packed, jnp.pad(old_weights.T, ((0, depth - classes), (0, 0))))[:classes]

    new_weights = old_weights + change.T
    taken = lax.dot_general(
        change, features, (((1,), (0,)), ((), ())), precision=HIGHEST, preferred_element_type=jnp.float32
    )
    return residual - taken.T, new_weights[None]


def solution(mesh):
    return jax.shard_map(
        body,
        mesh=mesh,
        in_specs=(
            P(("rows", "feat"), None),
            P(("rows", "feat"), None),
            P("feat", None, None),
            P("feat", None),
            P("feat", None, None),
            P(),
        ),
        out_specs=(P(("rows", "feat"), None), P()),
        check_vma=False,
    )
```

time: 667 us -> 261 us (0.39)
  other arithmetic: 267 us -> 4.22 us
  waiting for transfers between devices: 261 us -> 0.02 us
  Pallas kernels: 0 us -> 220 us
  matrix products: 55.8 us -> 9.91 us
  local copies, waits for them, and re-layouts: 46.3 us -> 9.87 us
  blocking collectives: 8.38 us -> 0 us
    another operation x34 -> x0, other arithmetic: 252 us -> none  [the longest x30 168 us: body(): factor = jnp.linalg.cholesky(system)]
    pallas_call x0 -> x3, Pallas kernels: none -> 220 us  [the longest x1 116 us: body(): pl.pallas_call(functools.partial(solve_kernel, total_rows), out_shape=jax...]
    reduce_scatter x1 -> x0, waiting for transfers between devices: 95.5 us -> none  [body(): lax.psum_scatter(lax.dot_general(features, joined, (((0,), (0,)), ((), ()...]
    all_gather x1 -> x0, waiting for transfers between devices: 84.1 us -> none  [body(): summed = lax.all_gather(share_rows, 'rows', axis=0, tiled=True)]
    psum x2 -> x1, waiting for transfers between devices: 80.8 us -> 0.01 us  [body(): old_weights = lax.psum(local(weights), 'feat')]
    another operation x44 -> x0, matrix products: 40.3 us -> none  [the longest x14 26.5 us: body(): factor = jnp.linalg.cholesky(system)]
    another operation x70 -> x0, local copies, waits for them, and re-layouts: 33.8 us -> none
    psum x1 -> x0, blocking collectives: 8.38 us -> none  [from_root(): return lax.psum(block, axis)]
  transfers between devices with their start and end apart: 4 -> 1, of which waited for: 4 -> 0; matrix products, arithmetic and copies ran while one was open for 0% -> 6% of each run, Pallas kernels for 0% -> 40%
where the time goes in v1:
time: 261 us
  Pallas kernels  220 us (84%)
  between operations  16.9 us (6%)
  matrix products  9.91 us (4%)
  local copies, waits for them, and re-layouts  9.87 us (4%)
  other arithmetic  4.22 us (2%)
    pallas_call x1, Pallas kernels, body(): pl.pallas_call(functools.partial(solve_kernel, total_rows), out_shape=jax...  116 us
    pallas_call x2, Pallas kernels, summing_call(): pl.pallas_call(functools.partial(kernel, bits, plans), out_shape=jax.Shap...  104 us
    dot_general x1, matrix products, body(): lax.dot_general(spread[:inputs], samples, (((0,), (1,)), ((), ())), preci...  8.44 us
  transfers between devices with their start and end apart: 1, of which 0 were waited for; matrix products, arithmetic and copies ran while one was open for 6% of the time, Pallas kernels for 40%

profile of v1, /device:TPU:0, one launch (start us, length us, event | category | flops | bytes accessed | tf_op | source)
XLA Modules:
  0.0 260.6 jit_solution(7047064454367186426)
XLA Ops:
  7.2 0.0 copy-start
  7.2 0.0 copy-start.5
  7.2 0.0 all-reduce.4.cloned.1.call-start
  9.9 0.0 copy-done
  9.9 0.5 constant_dynamic-slice_fusion
  10.5 1.0 fusion.2
  11.5 0.0 all-reduce.4.cloned.1.call-update
  11.5 0.0 copy-done.5
  11.5 1.7 select_bitcast_fusion
  13.2 1.5 pad_maximum_fusion
  14.7 1.6 reshape.18.block_ref
  16.3 39.6 %shard_map.77 = f32[3584,128]{1,0:T(8,128)S(1)} custom-call(f32[3584,128]{1,0:T(8,128)S(1)} %reshape.18.block_ref), custom_call_target="tpu_custom_call" | custom-call | tf_op jit(solution)/shard_map/pallas_call | solution.py:140
  55.9 0.1 slice.17
  56.0 0.0 copy-start.4
  56.0 1.5 slice.18
  57.5 0.0 copy-done.4
  57.5 8.4 %fusion.1.features_ref = f32[1024,256]{1,0:T(8,128)S(1)} fusion(f32[440,1024]{1,0:T(8,128)} %slice.18, f32[256,440]{0,1:T(8,128)} %param.6, f32[1024]{0:T(1024)S(1)} %slice_bitcast_fusion), kind=kOutput, calls=%fused_computation.4 | convolution fusion | flops 1384644608 | bytes 3305472 | tf_op jit(solution)/shard_map/dot_general | solution.py:246
  66.0 64.1 %shard_map.78.packed_ref = f32[6144,128]{1,0:T(8,128)S(1)} custom-call(f32[1024,256]{1,0:T(8,128)S(1)} %fusion.1.features_ref, f32[152,256]{1,0:T(8,128)S(1)} %pad.8.targets_ref), custom_call_target="tpu_custom_call" | custom-call | tf_op jit(solution)/shard_map/pallas_call | solution.py:140
  130.1 0.0 copy-start.1
  130.1 1.6 copy-done.1
  131.7 0.0 all-reduce.4.cloned.1.call-done
  131.7 1.1 pad.9.weights_ref
  132.9 0.0 copy-start.2
  132.9 1.9 copy-done.2
  134.8 116.0 %shard_map.79 = f32[152,1024]{1,0:T(8,128)S(1)} custom-call(f32[6144,128]{1,0:T(8,128)S(1)} %copy-done.2, f32[152,1024]{1,0:T(8,128)S(1)} %pad.9.weights_ref), custom_call_target="tpu_custom_call" | custom-call | tf_op jit(solution)/shard_map/pallas_call | solution.py:263
  250.7 0.0 copy-start.3
  250.7 1.5 convolution_subtract_fusion
  252.2 0.0 copy-done.3
  252.2 0.1 fusion.3
  252.3 1.4 copy.9
  (4 shorter events, 0.0 us)
Async XLA Ops:
  7.2 2.8 %copy-start = (f32[2,1024,147]{1,0,2:T(2,128)S(1)}, f32[2,1024,147]{1,0,2:T(2,128)}, u32[]{:S(2)}) copy-start(f32[2,1024,147]{1,0,2:T(2,128)} %param.10) | copy-start | bytes 3612676
  7.2 4.3 %copy-start.5 = (f32[2,1024]{1,0:T(2,128)S(1)}, f32[2,1024]{1,0:T(2,128)}, u32[]{:S(2)}) copy-start(f32[2,1024]{1,0:T(2,128)} %param.9) | copy-start | bytes 24580
  7.2 124.6 %all-reduce.4.cloned.1.call-start = ((), (), s32[]{:S(2)}) async-start(), calls=%async_computation | async-start | bytes 1245184 | tf_op jit(solution)/shard_map/psum | solution.py:237
  56.0 1.5 copy-start.4
  130.1 1.7 copy-start.1
  132.9 1.9 copy-start.2
  250.7 1.5 copy-start.3
Sparse Core Ops, SparseCore 0:
  11.6 40.4 all-reduce.3

commit v2 on v1

--- a/solution.py
+++ b/solution.py
@@ -49,7 +49,7 @@
     pl.semaphore_wait(barrier, len(bits))
 
 
-def sum_over(plans, buf, recv, out, send_sems, recv_sems):
+def sum_over(plans, buf, recv, out, send_sems, recv_sems, alike=()):
     rows_of = lambda start, size: pl.ds(pl.multiple_of(start, 8), size)
     state = [(base, rows) for base, rows, _ in plans]
     landing = [base for base, _, _ in plans]
@@ -67,6 +67,9 @@
             name, partner, bit = peer(part, step)
             start, size = state[part]
             half = size // 2
+            state[part] = (start + bit * half, half)
+            if name in alike:
+                continue
             copy = pltpu.make_async_remote_copy(
                 src_ref=buf.at[rows_of(start + (1 - bit) * half, half)],
                 dst_ref=recv.at[pl.ds(landing[part], half)],
@@ -76,9 +79,8 @@
                 device_id_type=pl.DeviceIdType.MESH,
             )
             copy.start()
-            copies.append(copy)
-            state[part] = (start + bit * half, half)
-        for part, copy in enumerate(copies):
+            copies.append((part, copy))
+        for part, copy in copies:
             copy.wait()
             start, half = state[part]
             mine = rows_of(start, half)
@@ -111,7 +113,7 @@
 def spread_kernel(bits, plans, block_ref, out_ref, buf, recv, send_sems, recv_sems):
     greet(bits)
     buf[...] = block_ref[...]
-    sum_over(plans, buf, recv, out_ref, send_sems, recv_sems)
+    sum_over(plans, buf, recv, out_ref, send_sems, recv_sems, alike=("rows",))
 
 
 def gram_kernel(bits, plans, features_ref, targets_ref, out_ref, buf, recv, send_sems, recv_sems):
@@ -157,17 +159,39 @@
 def invert(block):
     size = block.shape[0]
     pieces = [block[8 * n:8 * n + 8, :] for n in range(size // 8)]
-    lane = lax.broadcasted_iota(jnp.int32, (1, size), 1)
-    sub = lax.broadcasted_iota(jnp.int32, (8, 1), 0)
-    for k in range(size):
-        home, at = k // 8, k % 8
-        row = pieces[home][at:at + 1, :]
-        inverse = 1.0 / row[:, k:k + 1]
-        scaled = row * inverse
-        factor = jnp.where(lane == k, 1.0 + inverse, scaled)
-        kept = jnp.where(lane == k, inverse, scaled)
-        pieces = [piece - piece[:, k:k + 1] * factor for piece in pieces]
-        pieces[home] = jnp.where(sub == at, kept, pieces[home])
+    lane = lax.broadcasted_iota(jnp.int32, (8, size), 1)
+    sub = lax.broadcasted_iota(jnp.int32, (8, size), 0)
+
+    def spread_lane(piece, k):
+        return jnp.broadcast_to(piece[:, k:k + 1], (8, size))
+
+    for home in range(size // 8):
+        first = 8 * home
+        strip = pieces[home]
+        square = [spread_lane(strip, first + q) for q in range(8)]
+        for q in range(8):
+            inverse = 1.0 / jnp.broadcast_to(square[q][q:q + 1, :], (8, size))
+            is_row = sub == q
+            col = square[q]
+            row = jnp.broadcast_to(strip[q:q + 1, :], (8, size)) * inverse
+            strip = jnp.where(is_row, row, strip - col * row)
+            strip = jnp.where(lane == first + q, jnp.where(is_row, inverse, -col * inverse), strip)
+            for m in range(8):
+                if m != q:
+                    entry = jnp.broadcast_to(square[m][q:q + 1, :], (8, size)) * inverse
+                    square[m] = jnp.where(is_row, entry, square[m] - col * entry)
+            square[q] = jnp.where(is_row, inverse, -col * inverse)
+        factor = jnp.where(lane == first + sub, strip + 1.0, strip)
+        rows = [jnp.broadcast_to(factor[q:q + 1, :], (8, size)) for q in range(8)]
+        for n in range(size // 8):
+            if n != home:
+                piece = pieces[n]
+                terms = [spread_lane(piece, first + q) * rows[q] for q in range(8)]
+                total = ((terms[0] + terms[1]) + (terms[2] + terms[3])) + (
+                    (terms[4] + terms[5]) + (terms[6] + terms[7])
+                )
+                pieces[n] = piece - total
+        pieces[home] = strip
     return jnp.concatenate(pieces, axis=0)
 
 
@@ -236,12 +260,18 @@
 
     old_weights = lax.psum(local(weights), "feat")
     tiles = width // LANES
-    spread_rows = round_up((inputs + 8) * tiles, 8 * 2 ** len(feat_bits))
+    orders = [
+        feat_bits + rows_bits,
+        feat_bits[:1] + rows_bits + feat_bits[1:],
+        feat_bits[:1] + rows_bits[1:] + feat_bits[1:] + rows_bits[:1],
+    ]
+    bits = feat_bits + rows_bits
+    spread_rows = round_up((inputs + 8) * tiles, 8 * 2 ** len(bits) * len(orders))
     basis = jnp.concatenate(
         [local(projections), jnp.broadcast_to(local(phases)[None], (8, width))], axis=0
     ).reshape(-1, LANES)
     basis = jnp.pad(basis, ((0, spread_rows - basis.shape[0]), (0, 0)))
-    spread = summing_call(spread_kernel, feat_bits, [feat_bits], spread_rows, [basis], 1)
+    spread = summing_call(spread_kernel, bits, orders, spread_rows, [basis], 1)
     spread = spread[:(inputs + 8) * tiles].reshape(inputs + 8, width)
     projected = lax.dot_general(
         spread[:inputs], samples, (((0,), (1,)), ((), ())),
@@ -250,11 +280,6 @@
     features = root_two * jnp.cos(projected + spread[inputs][:, None])
     targets = jnp.pad(residual.T, ((0, depth - classes), (0, 0)))
 
-    orders = [
-        feat_bits + rows_bits,
-        feat_bits[:1] + rows_bits[:1] + feat_bits[1:] + rows_bits[1:][::-1],
-    ]
-    bits = feat_bits + rows_bits
     sum_rows = round_up(
         tiles * (tiles + 1) // 2 * LANES + tiles * depth, 8 * 2 ** len(bits) * len(orders)
     )

time: 261 us -> 208 us (0.80)
  Pallas kernels: 220 us -> 165 us
  local copies, waits for them, and re-layouts: 9.87 us -> 13.8 us
    pallas_call x1, Pallas kernels: 116 us -> 60.9 us  [body(): pl.pallas_call(functools.partial(solve_kernel, total_rows), out_shape=jax...]
  transfers between devices with their start and end apart: 1 -> 1, of which waited for: 0 -> 0; matrix products, arithmetic and copies ran while one was open for 6% -> 8% of each run, Pallas kernels for 40% -> 50%
where the time goes in v2:
time: 208 us
  Pallas kernels  165 us (79%)
  between operations  16.9 us (8%)
  local copies, waits for them, and re-layouts  13.8 us (7%)
  matrix products  9.77 us (5%)
  other arithmetic  2.88 us (1%)
    pallas_call x2, Pallas kernels, summing_call(): pl.pallas_call(functools.partial(kernel, bits, plans), out_shape=jax.Shap...  104 us
    pallas_call x1, Pallas kernels, body(): pl.pallas_call(functools.partial(solve_kernel, total_rows), out_shape=jax...  60.9 us
    dot_general x1, matrix products, body(): lax.dot_general(spread[:inputs], samples, (((0,), (1,)), ((), ())), preci...  8.31 us
    unnamed x15, local copies, waits for them, and re-layouts  4.99 us
  transfers between devices with their start and end apart: 1, of which 0 were waited for; matrix products, arithmetic and copies ran while one was open for 8% of the time, Pallas kernels for 50%

profile of v2, /device:TPU:0, one launch (start us, length us, event | category | flops | bytes accessed | tf_op | source)
XLA Modules:
  0.0 208.1 jit_solution(7637170453760936068)
XLA Ops:
  7.2 0.0 copy-start
  7.2 0.0 copy-start.6
  7.2 0.0 all-reduce.5.cloned.1.call-start
  9.9 0.0 copy-done
  9.9 0.5 constant_dynamic-slice_fusion
  10.5 1.0 fusion.2
  11.5 0.0 all-reduce.5.cloned.1.call-update
  11.5 0.0 copy-done.6
  11.5 1.7 select_bitcast_fusion
  13.2 0.1 pad_maximum_fusion
  13.3 1.5 reshape.18
  14.9 1.6 pad.12.block_ref
  16.5 42.2 %shard_map.77 = f32[3840,128]{1,0:T(8,128)S(1)} custom-call(f32[3840,128]{1,0:T(8,128)S(1)} %pad.12.block_ref), custom_call_target="tpu_custom_call" | custom-call | tf_op jit(solution)/shard_map/pallas_call | solution.py:142
  58.7 0.0 copy-start.4
  58.7 1.4 slice.20
  60.0 0.0 copy-done.4
  60.1 0.0 copy-start.5
  60.1 2.7 %slice.21 = f32[440,1024]{1,0:T(8,128)} reshape(f32[3520,128]{1,0:T(8,128)} %slice.20) | data formatting | bytes 3604480 | tf_op jit(solution)/shard_map/slice | solution.py:277
  62.7 0.0 copy-done.5
  62.7 8.3 %fusion.1.features_ref = f32[1024,256]{1,0:T(8,128)S(1)} fusion(f32[440,1024]{1,0:T(8,128)} %slice.21, f32[256,440]{0,1:T(8,128)S(1)} %copy-done.5, f32[1024]{0:T(1024)S(1)} %slice_bitcast_fusion), kind=kOutput, calls=%fused_computation.4 | convolution fusion | flops 1384644608 | bytes 3305472 | tf_op jit(solution)/shard_map/dot_general | solution.py:276
  71.1 61.6 %shard_map.78.packed_ref = f32[6144,128]{1,0:T(8,128)S(1)} custom-call(f32[1024,256]{1,0:T(8,128)S(1)} %fusion.1.features_ref, f32[152,256]{1,0:T(8,128)S(1)} %pad.13.targets_ref), custom_call_target="tpu_custom_call" | custom-call | tf_op jit(solution)/shard_map/pallas_call | solution.py:142
  132.7 0.0 copy-start.1
  132.7 1.6 copy-done.1
  134.4 0.0 all-reduce.5.cloned.1.call-done
  134.4 1.1 pad.14.weights_ref
  135.5 0.0 copy-start.2
  135.5 1.9 copy-done.2
  137.4 60.9 %shard_map.79 = f32[152,1024]{1,0:T(8,128)S(1)} custom-call(f32[6144,128]{1,0:T(8,128)S(1)} %copy-done.2, f32[152,1024]{1,0:T(8,128)S(1)} %pad.14.weights_ref), custom_call_target="tpu_custom_call" | custom-call | tf_op jit(solution)/shard_map/pallas_call | solution.py:288
  198.3 0.0 copy-start.3
  198.3 1.5 convolution_subtract_fusion
  199.7 0.0 copy-done.3
  199.7 0.1 fusion.3
  199.8 1.4 copy.9
  (4 shorter events, 0.0 us)
Async XLA Ops:
  7.2 2.8 %copy-start = (f32[2,1024,147]{1,0,2:T(2,128)S(1)}, f32[2,1024,147]{1,0,2:T(2,128)}, u32[]{:S(2)}) copy-start(f32[2,1024,147]{1,0,2:T(2,128)} %param.10) | copy-start | bytes 3612676
  7.2 4.3 %copy-start.6 = (f32[2,1024]{1,0:T(2,128)S(1)}, f32[2,1024]{1,0:T(2,128)}, u32[]{:S(2)}) copy-start(f32[2,1024]{1,0:T(2,128)} %param.9) | copy-start | bytes 24580
  7.2 127.2 %all-reduce.5.cloned.1.call-start = ((), (), s32[]{:S(2)}) async-start(), calls=%async_computation | async-start | bytes 1245184 | tf_op jit(solution)/shard_map/psum | solution.py:261
  58.7 1.4 copy-start.4
  60.1 2.7 %copy-start.5 = (f32[256,440]{0,1:T(8,128)S(1)}, f32[256,440]{0,1:T(8,128)}, u32[]{:S(2)}) copy-start(f32[256,440]{0,1:T(8,128)} %param.6) | copy-start | bytes 1351684
  132.7 1.6 copy-start.1
  135.5 1.9 copy-start.2
  198.3 1.5 copy-start.3
Sparse Core Ops, SparseCore 0:
  11.6 38.5 all-reduce.4

commit v3 on v2

--- a/solution.py
+++ b/solution.py
@@ -49,7 +49,7 @@
     pl.semaphore_wait(barrier, len(bits))
 
 
-def sum_over(plans, buf, recv, out, send_sems, recv_sems, alike=()):
+def sum_over(plans, buf, recv, out, send_sems, recv_sems, first, alike=()):
     rows_of = lambda start, size: pl.ds(pl.multiple_of(start, 8), size)
     state = [(base, rows) for base, rows, _ in plans]
     landing = [base for base, _, _ in plans]
@@ -61,78 +61,103 @@
         bit = (me // stride) % 2
         return name, me + stride * (1 - 2 * bit), bit
 
+    def halve(part, step):
+        name, partner, bit = peer(part, step)
+        start, size = state[part]
+        half = size // 2
+        state[part] = (start + bit * half, half)
+        if name in alike:
+            return None
+        copy = pltpu.make_async_remote_copy(
+            src_ref=buf.at[rows_of(start + (1 - bit) * half, half)],
+            dst_ref=recv.at[pl.ds(landing[part], half)],
+            send_sem=send_sems.at[0, part, step],
+            recv_sem=recv_sems.at[0, part, step],
+            device_id={name: partner},
+            device_id_type=pl.DeviceIdType.MESH,
+        )
+        copy.start()
+        return copy
+
+    def double(part, step):
+        name, partner, bit = peer(part, step)
+        start, size = state[part]
+        mine = rows_of(start, size)
+        copy = pltpu.make_async_remote_copy(
+            src_ref=out.at[mine],
+            dst_ref=out.at[mine],
+            send_sem=send_sems.at[1, part, step],
+            recv_sem=recv_sems.at[1, part, step],
+            device_id={name: partner},
+            device_id_type=pl.DeviceIdType.MESH,
+        )
+        copy.start()
+        state[part] = (start - bit * size, size * 2)
+        return copy
+
+    def finish(part, step, copy):
+        if copy is None:
+            return
+        copy.wait()
+        start, half = state[part]
+        mine = rows_of(start, half)
+        buf[mine, :] = buf[mine, :] + recv[pl.ds(landing[part], half), :]
+        landing[part] += half
+
+    parts = range(len(plans))
+    copies = [first(part, lambda part=part: halve(part, 0)) for part in parts]
     for step in range(count):
-        copies = []
-        for part in range(len(plans)):
-            name, partner, bit = peer(part, step)
-            start, size = state[part]
-            half = size // 2
-            state[part] = (start + bit * half, half)
-            if name in alike:
-                continue
-            copy = pltpu.make_async_remote_copy(
-                src_ref=buf.at[rows_of(start + (1 - bit) * half, half)],
-                dst_ref=recv.at[pl.ds(landing[part], half)],
-                send_sem=send_sems.at[0, part, step],
-                recv_sem=recv_sems.at[0, part, step],
-                device_id={name: partner},
-                device_id_type=pl.DeviceIdType.MESH,
-            )
-            copy.start()
-            copies.append((part, copy))
-        for part, copy in copies:
-            copy.wait()
-            start, half = state[part]
-            mine = rows_of(start, half)
-            buf[mine, :] = buf[mine, :] + recv[pl.ds(landing[part], half), :]
-            landing[part] += half
-    for start, size in state:
-        mine = rows_of(start, size)
-        out[mine, :] = buf[mine, :]
+        for part in parts:
+            finish(part, step, copies[part])
+            if step + 1 < count:
+                copies[part] = halve(part, step + 1)
+            else:
+                start, size = state[part]
+                mine = rows_of(start, size)
+                out[mine, :] = buf[mine, :]
+                copies[part] = double(part, count - 1)
     for step in reversed(range(count)):
-        copies = []
-        for part in range(len(plans)):
-            name, partner, bit = peer(part, step)
-            start, size = state[part]
-            mine = rows_of(start, size)
-            copy = pltpu.make_async_remote_copy(
-                src_ref=out.at[mine],
-                dst_ref=out.at[mine],
-                send_sem=send_sems.at[1, part, step],
-                recv_sem=recv_sems.at[1, part, step],
-                device_id={name: partner},
-                device_id_type=pl.DeviceIdType.MESH,
-            )
-            copy.start()
-            copies.append(copy)
-            state[part] = (start - bit * size, size * 2)
-        for copy in copies:
-            copy.wait()
+        for part in parts:
+            copies[part].wait()
+            if step > 0:
+                copies[part] = double(part, step - 1)
 
 
 def spread_kernel(bits, plans, block_ref, out_ref, buf, recv, send_sems, recv_sems):
     greet(bits)
     buf[...] = block_ref[...]
-    sum_over(plans, buf, recv, out_ref, send_sems, recv_sems, alike=("rows",))
-
-
-def gram_kernel(bits, plans, features_ref, targets_ref, out_ref, buf, recv, send_sems, recv_sems):
+    sum_over(plans, buf, recv, out_ref, send_sems, recv_sems, lambda part, go: go(), alike=("rows",))
+
+
+def gram_kernel(bits, plans, features_ref, targets_ref, pull_ref, out_ref, buf, recv, send_sems, recv_sems):
     greet(bits)
     tiles = features_ref.shape[0] // LANES
-    at = 0
-    for i in range(tiles):
-        panel = dot_nt(features_ref[i * LANES:(i + 1) * LANES, :], features_ref[:(i + 1) * LANES, :])
-        for j in range(i + 1):
-            buf[at:at + LANES, :] = panel[:, j * LANES:(j + 1) * LANES]
-            at += LANES
-    cross = dot_nt(targets_ref[...], features_ref[...])
-    depth = cross.shape[0]
-    for j in range(tiles):
-        buf[at:at + depth, :] = cross[:, j * LANES:(j + 1) * LANES]
-        at += depth
-    if at < buf.shape[0]:
-        buf[at:, :] = jnp.zeros((buf.shape[0] - at, LANES), jnp.float32)
-    sum_over(plans, buf, recv, out_ref, send_sems, recv_sems)
+    depth = targets_ref.shape[0]
+    done = [0, 0]
+
+    def fill(part, go):
+        end = plans[part][0] + plans[part][1]
+        while done[0] < end:
+            i, at = done[1], done[0]
+            if i < tiles:
+                panel = dot_nt(
+                    features_ref[i * LANES:(i + 1) * LANES, :], features_ref[:(i + 1) * LANES, :]
+                )
+                for j in range(i + 1):
+                    buf[at:at + LANES, :] = panel[:, j * LANES:(j + 1) * LANES]
+                    at += LANES
+            elif i == tiles:
+                cross = dot_nt(targets_ref[...], features_ref[...]) + pull_ref[...]
+                for j in range(tiles):
+                    buf[at:at + depth, :] = cross[:, j * LANES:(j + 1) * LANES]
+                    at += depth
+            else:
+                buf[at:, :] = jnp.zeros((buf.shape[0] - at, LANES), jnp.float32)
+                at = buf.shape[0]
+            done[:] = [at, i + 1]
+        return go()
+
+    sum_over(plans, buf, recv, out_ref, send_sems, recv_sems, fill)
 
 
 def summing_call(kernel, bits, orders, rows, operands, collective_id):
@@ -195,9 +220,8 @@
     return jnp.concatenate(pieces, axis=0)
 
 
-def solve_kernel(total_rows, packed_ref, weights_ref, change_ref, panels, diagonal_inverse):
-    width = weights_ref.shape[1]
-    depth = weights_ref.shape[0]
+def solve_kernel(total_rows, packed_ref, change_ref, panels, diagonal_inverse):
+    depth, width = change_ref.shape
     tiles = width // LANES
     scale = 1.0 / total_rows
     eye = (
@@ -213,9 +237,7 @@
             panels[j, i * LANES:(i + 1) * LANES, :] = block
             at += LANES
     for j in range(tiles):
-        panels[j, width:, :] = (
-            packed_ref[at:at + depth, :] * scale - penalty * weights_ref[:, j * LANES:(j + 1) * LANES]
-        )
+        panels[j, width:, :] = packed_ref[at:at + depth, :] * scale
         at += depth
 
     def eliminate(j):
@@ -258,7 +280,7 @@
         block = lax.dynamic_index_in_dim(array, slot, 0, False)
         return jnp.where(mine, block, jnp.zeros_like(block))
 
-    old_weights = lax.psum(local(weights), "feat")
+    own_weights = local(weights)
     tiles = width // LANES
     orders = [
         feat_bits + rows_bits,
@@ -280,22 +302,30 @@
     features = root_two * jnp.cos(projected + spread[inputs][:, None])
     targets = jnp.pad(residual.T, ((0, depth - classes), (0, 0)))
 
+    orders = orders * 2
+    pull = jnp.where(lax.axis_index("rows") == 0, -penalty * total_rows * own_weights.T, 0.0)
+    pull = jnp.pad(pull, ((0, depth - classes), (0, 0)))
     sum_rows = round_up(
         tiles * (tiles + 1) // 2 * LANES + tiles * depth, 8 * 2 ** len(bits) * len(orders)
     )
-    packed = summing_call(gram_kernel, bits, orders, sum_rows, [features, targets], 2)
+    packed = summing_call(gram_kernel, bits, orders, sum_rows, [features, targets, pull], 2)
+    own_weights, packed = lax.optimization_barrier((own_weights, packed))
+    old_weights = lax.psum(own_weights, "feat")
 
     change = pl.pallas_call(
         functools.partial(solve_kernel, total_rows),
         out_shape=jax.ShapeDtypeStruct((depth, width), jnp.float32),
-        in_specs=[pl.BlockSpec(memory_space=pltpu.VMEM)] * 2,
+        in_specs=[pl.BlockSpec(memory_space=pltpu.VMEM)],
         out_specs=pl.BlockSpec(memory_space=pltpu.VMEM),
         scratch_shapes=[
             pltpu.VMEM((tiles, width + depth, LANES), jnp.float32),
             pltpu.VMEM((LANES, LANES), jnp.float32),
         ],
         compiler_params=pltpu.CompilerParams(vmem_limit_bytes=VMEM_LIMIT),
-    )(packed, jnp.pad(old_weights.T, ((0, depth - classes), (0, 0))))[:classes]
+        cost_estimate=pl.CostEstimate(
+            flops=12 * width * width * (width // 3 + depth), bytes_accessed=2 * packed.size * 4, transcendentals=0
+        ),
+    )(packed)[:classes]
 
     new_weights = old_weights + change.T
     taken = lax.dot_general(

time: 208 us -> 186 us (0.89)
  Pallas kernels: 165 us -> 145 us
  local copies, waits for them, and re-layouts: 13.8 us -> 10.4 us
    pallas_call x2, Pallas kernels: 104 us -> 84 us  [summing_call(): pl.pallas_call(functools.partial(kernel, bits, plans), out_shape=jax.Shap...]
    slice x2, local copies, waits for them, and re-layouts: 4.02 us -> 1.63 us  [body(): spread[:inputs]]
    unnamed x15 -> x13, local copies, waits for them, and re-layouts: 4.99 us -> 4.99 us
  transfers between devices with their start and end apart: 1 -> 1, of which waited for: 0 -> 0; matrix products, arithmetic and copies ran while one was open for 8% -> 1% of each run, Pallas kernels for 50% -> 33%
where the time goes in v3:
time: 186 us
  Pallas kernels  145 us (78%)
  between operations  16.9 us (9%)
  local copies, waits for them, and re-layouts  10.4 us (6%)
  matrix products  9.78 us (5%)
  other arithmetic  4.19 us (2%)
    pallas_call x2, Pallas kernels, summing_call(): pl.pallas_call(functools.partial(kernel, bits, plans), out_shape=jax.Shap...  84 us
    pallas_call x1, Pallas kernels, body(): pl.pallas_call(functools.partial(solve_kernel, total_rows), out_shape=jax...  60.8 us
    dot_general x1, matrix products, body(): lax.dot_general(spread[:inputs], samples, (((0,), (1,)), ((), ())), preci...  8.32 us
    unnamed x13, local copies, waits for them, and re-layouts  4.99 us
  transfers between devices with their start and end apart: 1, of which 0 were waited for; matrix products, arithmetic and copies ran while one was open for 1% of the time, Pallas kernels for 33%

profile of v3, /device:TPU:0, one launch (start us, length us, event | category | flops | bytes accessed | tf_op | source)
XLA Modules:
  0.0 186.1 jit_solution(6265385905067251464)
XLA Ops:
  7.2 0.0 copy-start
  7.2 0.0 all-reduce.5.cloned.1.call-start
  9.9 0.0 copy-start.5
  9.9 1.7 select_bitcast_fusion
  11.6 0.0 copy-done.5
  11.7 0.1 pad_maximum_fusion
  11.8 1.5 reshape.18
  13.3 1.6 pad.12.block_ref
  14.9 34.6 %shard_map.77 = f32[3840,128]{1,0:T(8,128)S(1)} custom-call(f32[3840,128]{1,0:T(8,128)S(1)} %pad.12.block_ref), custom_call_target="tpu_custom_call" | custom-call | tf_op jit(solution)/shard_map/pallas_call | solution.py:167
  49.6 0.1 slice.20
  49.7 1.5 slice.21
  51.2 0.0 copy-done
  51.2 0.5 constant_dynamic-slice_fusion
  51.7 0.0 copy-start.3
  51.8 0.0 copy-start.4
  51.8 1.0 fusion.2
  52.8 0.2 select_bitcast_fusion.1
  52.9 0.1 pad.14.pull_ref
  53.0 0.0 copy-done.3
  53.0 0.0 copy-done.4
  53.0 8.3 %fusion.1.features_ref = f32[1024,256]{1,0:T(8,128)S(1)} fusion(f32[440,1024]{1,0:T(8,128)} %slice.21, f32[256,440]{0,1:T(8,128)S(1)} %copy-done.4, f32[1024]{0:T(1024)S(1)} %slice_bitcast_fusion), kind=kOutput, calls=%fused_computation.4 | convolution fusion | flops 1384644608 | bytes 3305472 | tf_op jit(solution)/shard_map/dot_general | solution.py:298
  61.4 49.4 %shard_map.78.packed_ref = f32[6144,128]{1,0:T(8,128)S(1)} custom-call(f32[1024,256]{1,0:T(8,128)S(1)} %fusion.1.features_ref, f32[152,256]{1,0:T(8,128)S(1)} %pad.13.targets_ref, f32[152,1024]{1,0:T(8,128)S(1)} %pad.14.pull_ref), custom_call_target="tpu_custom_call" | custom-call | tf_op jit(solution)/shard_map/pallas_call | solution.py:167
  110.8 0.0 copy-start.1
  110.8 1.6 copy-done.1
  112.4 0.0 all-reduce.5.cloned.1.call-update
  112.4 0.0 copy-start.2
  112.5 1.9 %copy-done.2 = f32[6144,128]{1,0:T(8,128)S(1)} copy-done((f32[6144,128]{1,0:T(8,128)S(1)}, f32[6144,128]{1,0:T(8,128)}, u32[]{:S(2)}) %copy-start.2) | copy-done | bytes 3145752
  114.3 60.8 %shard_map.79 = f32[152,1024]{1,0:T(8,128)S(1)} custom-call(f32[6144,128]{1,0:T(8,128)S(1)} %copy-done.2), custom_call_target="tpu_custom_call" | custom-call | flops 6203375616 | bytes 6291456 | tf_op jit(solution)/shard_map/pallas_call | solution.py:315
  175.2 1.5 convolution_subtract_fusion
  176.6 0.0 all-reduce.5.cloned.1.call-done
  176.6 1.2 fusion.3
  177.8 1.4 copy.9
  (4 shorter events, 0.0 us)
Async XLA Ops:
  7.2 44.0 %copy-start = (f32[2,1024,147]{1,0,2:T(2,128)S(1)}, f32[2,1024,147]{1,0,2:T(2,128)}, u32[]{:S(2)}) copy-start(f32[2,1024,147]{1,0,2:T(2,128)} %param.10) | copy-start | bytes 3612676
  7.2 169.4 %all-reduce.5.cloned.1.call-start = ((), (), s32[]{:S(2)}) async-start(), calls=%async_computation | async-start | bytes 1245184 | tf_op jit(solution)/shard_map/psum | solution.py:313
  9.9 1.7 copy-start.5
  51.7 1.3 copy-start.3
  51.8 1.3 copy-start.4
  110.8 1.7 copy-start.1
  112.4 1.9 %copy-start.2 = (f32[6144,128]{1,0:T(8,128)S(1)}, f32[6144,128]{1,0:T(8,128)}, u32[]{:S(2)}) copy-start(f32[6144,128]{1,0:T(8,128)} %copy-done.1) | copy-start | bytes 9437188
Sparse Core Ops, SparseCore 0:
  112.6 32.2 all-reduce.4

commit v4 on v3

--- a/solution.py
+++ b/solution.py
@@ -243,10 +243,12 @@
     def eliminate(j):
         below = (j + 1) * LANES
         ratio = dot_nn(panels[j, below:, :], diagonal_inverse[...])
-        for k in range(j + 1, tiles):
-            panels[k, k * LANES:, :] = panels[k, k * LANES:, :] - dot_nt(
-                ratio[(k - j - 1) * LANES:, :], panels[j, k * LANES:(k + 1) * LANES, :]
-            )
+        for k in range(j + 1, tiles, 2):
+            last = min(k + 2, tiles)
+            delta = dot_nt(ratio[(k - j - 1) * LANES:, :], panels[j, k * LANES:last * LANES, :])
+            for n in range(k, last):
+                skip = (n - k) * LANES
+                panels[n, n * LANES:, :] = panels[n, n * LANES:, :] - delta[skip:, skip:skip + LANES]
         panels[j, below:, :] = ratio
 
     def step(j, carry):

time: 186 us -> 181 us (0.973)
  Pallas kernels: 145 us -> 139 us
    pallas_call x1, Pallas kernels: 60.8 us -> 55.2 us  [body(): pl.pallas_call(functools.partial(solve_kernel, total_rows), out_shape=jax...]
  transfers between devices with their start and end apart: 1 -> 1, of which waited for: 0 -> 0; matrix products, arithmetic and copies ran while one was open for 1% -> 1% of each run, Pallas kernels for 33% -> 31%
where the time goes in v4:
time: 181 us; the launch traced here: 180 us
  Pallas kernels  139 us (77%)
  between operations  16.9 us (9%)
  local copies, waits for them, and re-layouts  10.4 us (6%)
  matrix products  9.78 us (5%)
  other arithmetic  4.19 us (2%)
    pallas_call x2, Pallas kernels, summing_call(): pl.pallas_call(functools.partial(kernel, bits, plans), out_shape=jax.Shap...  84 us
    pallas_call x1, Pallas kernels, body(): pl.pallas_call(functools.partial(solve_kernel, total_rows), out_shape=jax...  55.2 us
    dot_general x1, matrix products, body(): lax.dot_general(spread[:inputs], samples, (((0,), (1,)), ((), ())), preci...  8.32 us
    unnamed x13, local copies, waits for them, and re-layouts  4.99 us
  transfers between devices with their start and end apart: 1, of which 0 were waited for; matrix products, arithmetic and copies ran while one was open for 1% of the time, Pallas kernels for 31%

profile of v4, /device:TPU:0, one launch (start us, length us, event | category | flops | bytes accessed | tf_op | source)
XLA Modules:
  0.0 180.5 jit_solution(12551546754503752561)
XLA Ops:
  7.2 0.0 copy-start
  7.2 0.0 all-reduce.5.cloned.1.call-start
  9.9 0.0 copy-start.5
  9.9 1.7 select_bitcast_fusion
  11.6 0.0 copy-done.5
  11.7 0.1 pad_maximum_fusion
  11.8 1.5 reshape.18
  13.3 1.6 pad.12.block_ref
  14.9 34.6 %shard_map.77 = f32[3840,128]{1,0:T(8,128)S(1)} custom-call(f32[3840,128]{1,0:T(8,128)S(1)} %pad.12.block_ref), custom_call_target="tpu_custom_call" | custom-call | tf_op jit(solution)/shard_map/pallas_call | solution.py:167
  49.6 0.1 slice.20
  49.7 1.5 slice.21
  51.2 0.0 copy-done
  51.2 0.5 constant_dynamic-slice_fusion
  51.7 0.0 copy-start.3
  51.8 0.0 copy-start.4
  51.8 1.0 fusion.2
  52.8 0.2 select_bitcast_fusion.1
  52.9 0.1 pad.14.pull_ref
  53.0 0.0 copy-done.3
  53.0 0.0 copy-done.4
  53.0 8.3 %fusion.1.features_ref = f32[1024,256]{1,0:T(8,128)S(1)} fusion(f32[440,1024]{1,0:T(8,128)} %slice.21, f32[256,440]{0,1:T(8,128)S(1)} %copy-done.4, f32[1024]{0:T(1024)S(1)} %slice_bitcast_fusion), kind=kOutput, calls=%fused_computation.4 | convolution fusion | flops 1384644608 | bytes 3305472 | tf_op jit(solution)/shard_map/dot_general | solution.py:300
  61.4 49.4 %shard_map.78.packed_ref = f32[6144,128]{1,0:T(8,128)S(1)} custom-call(f32[1024,256]{1,0:T(8,128)S(1)} %fusion.1.features_ref, f32[152,256]{1,0:T(8,128)S(1)} %pad.13.targets_ref, f32[152,1024]{1,0:T(8,128)S(1)} %pad.14.pull_ref), custom_call_target="tpu_custom_call" | custom-call | tf_op jit(solution)/shard_map/pallas_call | solution.py:167
  110.8 0.0 copy-start.1
  110.8 1.6 copy-done.1
  112.4 0.0 all-reduce.5.cloned.1.call-update
  112.4 0.0 copy-start.2
  112.5 1.9 %copy-done.2 = f32[6144,128]{1,0:T(8,128)S(1)} copy-done((f32[6144,128]{1,0:T(8,128)S(1)}, f32[6144,128]{1,0:T(8,128)}, u32[]{:S(2)}) %copy-start.2) | copy-done | bytes 3145752
  114.3 55.2 %shard_map.79 = f32[152,1024]{1,0:T(8,128)S(1)} custom-call(f32[6144,128]{1,0:T(8,128)S(1)} %copy-done.2), custom_call_target="tpu_custom_call" | custom-call | flops 6203375616 | bytes 6291456 | tf_op jit(solution)/shard_map/pallas_call | solution.py:317
  169.5 1.5 convolution_subtract_fusion
  171.0 0.0 all-reduce.5.cloned.1.call-done
  171.0 1.2 fusion.3
  172.2 1.4 copy.9
  (4 shorter events, 0.0 us)
Async XLA Ops:
  7.2 44.0 %copy-start = (f32[2,1024,147]{1,0,2:T(2,128)S(1)}, f32[2,1024,147]{1,0,2:T(2,128)}, u32[]{:S(2)}) copy-start(f32[2,1024,147]{1,0,2:T(2,128)} %param.10) | copy-start | bytes 3612676
  7.2 163.8 %all-reduce.5.cloned.1.call-start = ((), (), s32[]{:S(2)}) async-start(), calls=%async_computation | async-start | bytes 1245184 | tf_op jit(solution)/shard_map/psum | solution.py:315
  9.9 1.7 copy-start.5
  51.7 1.3 copy-start.3
  51.8 1.3 copy-start.4
  110.8 1.7 copy-start.1
  112.4 1.9 %copy-start.2 = (f32[6144,128]{1,0:T(8,128)S(1)}, f32[6144,128]{1,0:T(8,128)}, u32[]{:S(2)}) copy-start(f32[6144,128]{1,0:T(8,128)} %copy-done.1) | copy-start | bytes 9437188
Sparse Core Ops, SparseCore 0:
  112.6 32.2 all-reduce.4
